TPU v7x, 32 devices: a whole 2x2x4 slice. The times are simulated.
32 devices in a mesh: space: 8 (over y, x, core), date: 4 (over z).
Axes of the slice: x: 2, y: 2, z: 4, core: 2. Of those that a mesh axis runs over, the one named last changes fastest.
Arguments:
- scene_panels: float32 [4, 64, 48, 384], P('date', 'space'), may hold values from -25 to 25
- panel_owner: int32 [4, 64], P('date'), may hold values from 0 to 7, as said below
- panel_offset: int32 [4, 64], P('date'), may hold values from 0 to 7, as said below
- panel_rows: int32 [4, 64], P('date'), may hold values from 24 to 48
- pair_used: int32 [4, 2], P('date'), may hold values 0 or 1
Outputs:
- correlation: float32 [4, 8, 2, 17, 17, 144], P('date', 'space')
Inputs may be any that keep to these rules, and one draw needn't show every extreme that they name: `panel_owner`: for each date, the 8 panels held by one index of space name each tile once. `panel_offset`: for each date and tile, the panels that name the tile carry each slot 0 to 7 once.
All inputs are finite; a program needn't handle non-finite values. No bound on the sum of `pair_used` on one device may be relied on, other than what follows from the above.
Results may differ from a plain program's by a relative error of at most 0.0028.
Values may be sent and summed in bfloat16 or wider, within the bound.
A program may use at most 64 MiB of HBM per device.

v0:
```python
import functools
import math

import jax
import jax.numpy as jnp
import ml_dtypes
import numpy as np
from jax import lax
from jax.experimental import pallas as pl
from jax.experimental.pallas import tpu as pltpu
from jax.sharding import PartitionSpec as P

CHIP = 32
SEARCH = 8
WALLIS = 10
FRAME = CHIP + 2 * SEARCH
LAGS = 2 * SEARCH + 1
HALF = FRAME // 2
WALLIS_FLOOR = 0.25
MATCH_FLOOR = 0.1
TILE = 384
COUNT = TILE // CHIP
CHIPS = COUNT * COUNT
GROUPS = 3
PER = COUNT // GROUPS
UPAD = 24
FIRST = 128 // COUNT
F32 = jnp.float32
BF16 = jnp.bfloat16

ROW_START = (0, 112, 224)
ROW_LEN = 160
COL_START = (0, 0, 128)
COL_LEN = (256, 384, 256)


def lane_of(v, cj):
    return v * COUNT + cj if v < FIRST else 128 + (v - FIRST) * COUNT + cj


def split_host(x):
    hi = x.astype(ml_dtypes.bfloat16)
    lo = (x - hi.astype(np.float64)).astype(ml_dtypes.bfloat16)
    return np.stack([hi, lo])


@functools.lru_cache(None)
def tables():
    j = np.arange(HALF)
    omega = 2.0 * math.pi * (j + 0.5) / FRAME

    def columns(lo, hi):
        out = np.zeros((TILE, GROUPS * 256))
        for cj in range(COUNT):
            g, q = divmod(cj, PER)
            for b in range(lo, hi):
                x = CHIP * cj + b - SEARCH
                if 0 <= x < TILE:
                    base = g * 256 + q * HALF
                    out[x, base : base + HALF] = np.cos(omega * (b - lo if lo else b))
                    out[x, base + 128 : base + 128 + HALF] = np.sin(omega * (b - lo if lo else b))
        return out

    def rows(lo, hi):
        out = np.zeros((GROUPS, 2 * PER * HALF, ROW_LEN))
        for ci in range(COUNT):
            h, q = divmod(ci, PER)
            for a in range(lo, hi):
                y = CHIP * ci + a - SEARCH
                if 0 <= y < TILE:
                    out[h, q * HALF : (q + 1) * HALF, y - ROW_START[h]] = np.cos(omega * (a - lo if lo else a))
                    base = PER * HALF + q * HALF
                    out[h, base : base + HALF, y - ROW_START[h]] = np.sin(omega * (a - lo if lo else a))
        return out

    back_rows = np.zeros((PER * UPAD, 2 * PER * HALF))
    for q in range(PER):
        for u in range(LAGS):
            back_rows[q * UPAD + u, q * HALF : (q + 1) * HALF] = np.cos(omega * u)
            base = PER * HALF + q * HALF
            back_rows[q * UPAD + u, base : base + HALF] = np.sin(omega * u)
    back_cols = np.zeros((GROUPS, 256, 256))
    for cj in range(COUNT):
        g, q = divmod(cj, PER)
        for v in range(LAGS):
            back_cols[g, q * HALF : (q + 1) * HALF, lane_of(v, cj)] = np.cos(omega * v)
            base = 128 + q * HALF
            back_cols[g, base : base + HALF, lane_of(v, cj)] = np.sin(omega * v)

    wide = np.zeros((2, TILE, 256))
    tall = np.zeros((2, COUNT * UPAD, TILE))
    for c in range(COUNT):
        for v in range(LAGS):
            start = CHIP * c + v - SEARCH
            wide[0, max(start, 0) : max(start + CHIP, 0), lane_of(v, c)] = 1
            tall[0, c * UPAD + v, max(start, 0) : max(start + CHIP, 0)] = 1
            wide[1, CHIP * c : CHIP * c + CHIP, lane_of(v, c)] = 1
            tall[1, c * UPAD + v, CHIP * c : CHIP * c + CHIP] = 1
    return (
        split_host(columns(SEARCH, SEARCH + CHIP)),
        split_host(columns(0, FRAME)),
        split_host(rows(SEARCH, SEARCH + CHIP)),
        split_host(rows(0, FRAME)),
        split_host(back_rows),
        split_host(back_cols),
        wide.astype(ml_dtypes.bfloat16),
        tall.astype(ml_dtypes.bfloat16),
    )


def dot(a, b):
    return jnp.dot(a, b, preferred_element_type=F32)


def split(x):
    hi = x.astype(BF16)
    return hi, (x - hi.astype(F32)).astype(BF16)


def split3(x):
    hi = x.astype(BF16)
    rest = x - hi.astype(F32)
    mid = rest.astype(BF16)
    return hi, mid, (rest - mid.astype(F32)).astype(BF16)


def boxed(x, box):
    a, b, c = split3(x)
    first = dot(box, a) + dot(box, b) + dot(box, c)
    a, b, c = split3(first)
    return dot(a, box) + dot(b, box) + dot(c, box)


def wallis(image):
    size = image.shape[0]
    i = lax.broadcasted_iota(jnp.int32, (size, size), 0)
    j = lax.broadcasted_iota(jnp.int32, (size, size), 1)
    box = jnp.where(jnp.abs(i - j) <= WALLIS, 1.0, 0.0).astype(BF16)

    def counts(k):
        return (jnp.minimum(k, WALLIS) + jnp.minimum(size - 1 - k, WALLIS) + 1).astype(F32)

    rows = counts(lax.broadcasted_iota(jnp.int32, (size, 1), 0))
    cols = counts(lax.broadcasted_iota(jnp.int32, (1, size), 1))
    inverse = (1.0 / rows) * (1.0 / cols)
    center = boxed(image, box) * inverse
    spread = boxed(image * image, box) * inverse - center * center
    return ((image - center) * lax.rsqrt(spread + WALLIS_FLOOR)).astype(BF16)


def wallis_kernel(image_ref, out_ref):
    out_ref[...] = wallis(image_ref[...])


def spectrum(x, cols_ref, rows_ref, store):
    parts = []
    for g in range(GROUPS):
        at = pl.ds(COL_START[g], COL_LEN[g])
        piece = x[:, COL_START[g] : COL_START[g] + COL_LEN[g]]
        lanes = pl.ds(g * 256, 256)
        z = dot(piece, cols_ref[0, at, lanes]) + dot(piece, cols_ref[1, at, lanes])
        hi, lo = split(z)
        for h in range(GROUPS):
            s = ROW_START[h]
            zh, zl = hi[s : s + ROW_LEN], lo[s : s + ROW_LEN]
            store[h, :, lanes] = dot(rows_ref[0, h], zh) + dot(rows_ref[0, h], zl) + dot(rows_ref[1, h], zh)


def powers(x, wide, tall):
    wide_f = x.astype(F32)
    hi, lo = split(wide_f * wide_f)
    hi, lo = split(dot(hi, wide) + dot(lo, wide))
    return dot(tall, hi) + dot(tall, lo)


def surfaces(ref_spec, frame_spec, ref_power, frame_power, used, back_rows, back_cols, match_ref):
    mid = PER * HALF
    area = float(CHIP * CHIP)
    for h in range(GROUPS):
        total = None
        for g in range(GROUPS):
            even, odd = pl.ds(g * 256, 128), pl.ds(g * 256 + 128, 128)
            top, low = pl.ds(0, mid), pl.ds(mid, mid)
            rcc, rcs = ref_spec[h, top, even], ref_spec[h, top, odd]
            rsc, rss = ref_spec[h, low, even], ref_spec[h, low, odd]
            wcc, wcs = frame_spec[h, top, even], frame_spec[h, top, odd]
            wsc, wss = frame_spec[h, low, even], frame_spec[h, low, odd]
            ap, bp, am, bm = rcc - rss, rsc + rcs, rcc + rss, rsc - rcs
            cp, dp, cm, dm = wcc - wss, wsc + wcs, wcc + wss, wsc - wcs
            pr, pi = ap * cp + bp * dp, bp * cp - ap * dp
            mr, mi = am * cm + bm * dm, bm * cm - am * dm
            upper = jnp.concatenate([pr + mr, mi - pi], axis=1)
            lower = jnp.concatenate([-(pi + mi), mr - pr], axis=1)
            hi, lo = split(jnp.concatenate([upper, lower], axis=0))
            y = dot(back_rows[0], hi) + dot(back_rows[0], lo) + dot(back_rows[1], hi)
            hi, lo = split(y)
            term = dot(hi, back_cols[0, g]) + dot(lo, back_cols[0, g]) + dot(hi, back_cols[1, g])
            total = term if total is None else total + term
        at = pl.ds(h * PER * UPAD, PER * UPAD)
        scale = 2.0 / (FRAME * FRAME) / area
        power = (ref_power[at, :] * (1.0 / area) + MATCH_FLOOR) * (frame_power[at, :] * (1.0 / area) + MATCH_FLOOR)
        match_ref[at, :] = total * (scale * used) * lax.rsqrt(power)


def arrange(match_ref, out_ref, k):
    lane = lax.broadcasted_iota(jnp.int32, (UPAD, 128), 1)
    for v in range(LAGS):
        start = lane_of(v, 0)
        tile, off = divmod(start, 128)
        first = jnp.zeros((UPAD, 128), F32)
        second = jnp.zeros((UPAD, 128), F32)
        for ci in range(COUNT):
            piece = match_ref[pl.ds(ci * UPAD, UPAD), pl.ds(tile * 128, 128)]
            turn = (COUNT * ci - off) % 128
            if turn:
                piece = pltpu.roll(piece, turn, 1)
            begin, end = COUNT * ci, COUNT * ci + COUNT
            if begin < 128:
                first = jnp.where((lane >= begin) & (lane < end), piece, first)
            if end > 128:
                second = jnp.where((lane >= begin - 128) & (lane < end - 128), piece, second)
        out_ref[k, :, v, pl.ds(0, 128)] = first[:LAGS]
        out_ref[k, :, v, pl.ds(128, CHIPS - 128)] = second[:LAGS, : CHIPS - 128]


def correlate_kernel(
    used_ref, own_ref, one_ref, two_ref,
    ref_cols, frame_cols, ref_rows, frame_rows, back_rows, back_cols, wide, tall,
    out_ref, ref_spec, frame_spec, ref_power, frame_power, match_ref,
):
    own = own_ref[...]
    spectrum(own, ref_cols, ref_rows, ref_spec)
    ref_power[...] = powers(own, wide[1], tall[1])
    for k, held in enumerate((one_ref, two_ref)):
        x = held[...]
        spectrum(x, frame_cols, frame_rows, frame_spec)
        frame_power[...] = powers(x, wide[0], tall[0])
        used = used_ref[k].astype(F32)
        surfaces(ref_spec, frame_spec, ref_power, frame_power, used, back_rows, back_cols, match_ref)
        arrange(match_ref, out_ref, k)


def shifted(x, axis, by):
    devices = lax.axis_size(axis)
    return lax.ppermute(x, axis, [(i, (i + by) % devices) for i in range(devices)])


def local(scene_panels, panel_owner, panel_offset, panel_rows, pair_used):
    tiles = lax.axis_size("space")
    here = lax.axis_index("space")
    panels = scene_panels[0]
    rows_each = panels.shape[1]
    width = panels.shape[2]
    owner = panel_owner[0].reshape(tiles, tiles)
    offset = panel_offset[0].reshape(tiles, tiles)
    valid = panel_rows[0].reshape(tiles, tiles)
    mine = owner[here]
    live = (jnp.arange(rows_each)[None, :] < valid[here][:, None]).astype(jnp.float32)
    masked = panels * live[:, :, None]
    targets = jnp.arange(tiles, dtype=jnp.int32)
    picks = jnp.sum(jnp.where(mine[None, :] == targets[:, None], targets[None, :], 0), axis=1)
    outgoing = masked[picks]
    incoming = lax.all_to_all(outgoing, "space", split_axis=0, concat_axis=0, tiled=True)
    slot_of = jnp.sum(jnp.where(owner == here, offset, 0), axis=1)
    order = jnp.sum(jnp.where(slot_of[None, :] == targets[:, None], targets[None, :], 0), axis=1)
    image = incoming[order].reshape(width, width)
    vmem = pl.BlockSpec(memory_space=pltpu.VMEM)
    filtered = pl.pallas_call(
        wallis_kernel,
        out_shape=jax.ShapeDtypeStruct((width, width), BF16),
        in_specs=[vmem],
        out_specs=vmem,
        compiler_params=pltpu.CompilerParams(vmem_limit_bytes=40 * 2**20),
    )(image)
    one = shifted(filtered, "date", 1)
    two = shifted(filtered, "date", 2)
    consts = [jnp.asarray(t) for t in tables()]
    shifts = pair_used.shape[1]
    out = pl.pallas_call(
        correlate_kernel,
        out_shape=jax.ShapeDtypeStruct((shifts, LAGS, LAGS, CHIPS), F32),
        in_specs=[pl.BlockSpec(memory_space=pltpu.SMEM)] + [vmem] * (3 + len(consts)),
        out_specs=vmem,
        scratch_shapes=[
            pltpu.VMEM((GROUPS, 2 * PER * HALF, GROUPS * 256), F32),
            pltpu.VMEM((GROUPS, 2 * PER * HALF, GROUPS * 256), F32),
            pltpu.VMEM((COUNT * UPAD, 256), F32),
            pltpu.VMEM((COUNT * UPAD, 256), F32),
            pltpu.VMEM((COUNT * UPAD, 256), F32),
        ],
        compiler_params=pltpu.CompilerParams(vmem_limit_bytes=40 * 2**20),
    )(pair_used[0], filtered, one, two, *consts)
    return out[None, None]


def solution(mesh):
    placed = (
        P("date", "space", None, None),
        P("date", None),
        P("date", None),
        P("date", None),
        P("date", None),
    )
    return jax.shard_map(
        local,
        mesh=mesh,
        in_specs=placed,
        out_specs=P("date", "space", None, None, None, None),
        check_vma=False,
    )
```

profile of v0, /device:TPU:19, one launch (start us, length us, event | category | flops | bytes accessed | tf_op | source)
XLA Modules:
  0.0 62.5 jit_solution(5454038847944970194)
XLA Ops:
  0.0 0.5 broadcast.79
  0.5 1.2 %reduce.10 = s32[64]{0:T(128)S(1)} reduce(s32[1,64]{1,0:T(1,128)} %param.14, s32[]{:T(128)} %broadcast.79), dimensions={0}, to_apply=%param.14.reduce_sub_computation.3 | reduce | bytes 516 | tf_op args[1]
  1.7 1.2 %reduce.9 = s32[64]{0:T(128)S(1)} reduce(s32[1,64]{1,0:T(1,128)} %param.16, s32[]{:T(128)} %broadcast.79), dimensions={0}, to_apply=%param.16.reduce_sub_computation.3 | reduce | bytes 516 | tf_op args[3]
  3.0 0.1 reshape_squeeze.10
  3.0 0.1 reshape_squeeze.9
  3.1 0.1 select_reduce_fusion.2
  3.3 0.1 fusion
  3.3 1.2 %bitcast_multiply_fusion = f32[8,48,384]{2,1,0:T(8,128)S(1)} fusion(f32[1,8,48,384]{3,2,1,0:T(8,128)} %param.13, f32[8,48]{1,0:T(8,128)S(1)} %fusion), kind=kLoop, calls=%fused_computation.2 | loop fusion | flops 147456 | bytes 1181184 | tf_op jit(solution)/shard_map/mul | solution.py:259
  4.5 0.0 copy-start.9
  4.5 0.0 copy-start.3
  4.6 1.4 %gather_fusion = f32[8,48,384]{2,1,0:T(8,128)} fusion(f32[8,48,384]{2,1,0:T(8,128)S(1)} %bitcast_multiply_fusion, s32[1024]{0:T(1024)S(1)} %pad_clamp_fusion.1), kind=kCustom, calls=%fused_computation | custom fusion | bytes 1179680 | tf_op jit(solution)/shard_map/gather | solution.py:262
  6.0 0.0 copy-start.1
  6.0 5.1 %all-to-all-start = ((f32[8,48,384]{2,1,0:T(8,128)}), f32[8,48,384]{2,1,0:T(8,128)}, u32[]{:S(2)}, u32[]{:S(2)}) async-start(f32[8,48,384]{2,1,0:T(8,128)} %gather_fusion), calls=%async_computation | async-start | bytes 1179648 | tf_op jit(solution)/shard_map/all_to_all | solution.py:263
  11.0 0.0 copy-done.9
  11.0 0.0 copy-start
  11.0 0.0 copy-start.8
  11.0 0.7 %reduce.11 = s32[64]{0:T(128)S(1)} reduce(s32[1,64]{1,0:T(1,128)S(1)} %copy-done.9, s32[]{:T(128)} %broadcast.79), dimensions={0}, to_apply=%param.15.reduce_sub_computation.3 | reduce | bytes 516 | tf_op args[2]
  11.7 0.1 reshape_squeeze.11
  11.8 0.1 select_reduce_fusion.1
  11.9 0.1 select_reduce_fusion
  12.0 8.0 %all-to-all-done = f32[8,48,384]{2,1,0:T(8,128)} async-done(((f32[8,48,384]{2,1,0:T(8,128)}), f32[8,48,384]{2,1,0:T(8,128)}, u32[]{:S(2)}, u32[]{:S(2)}) %all-to-all-start) | async-done | bytes 589856 | tf_op jit(solution)/shard_map/all_to_all | solution.py:263
  20.0 1.6 %gather_fusion.1 = f32[8,48,384]{2,1,0:T(8,128)S(1)} fusion(f32[8,48,384]{2,1,0:T(8,128)} %all-to-all-done, s32[1024]{0:T(1024)S(1)} %pad_clamp_fusion), kind=kCustom, calls=%fused_computation.1 | custom fusion | bytes 1179680 | tf_op jit(solution)/shard_map/gather | solution.py:266
  21.7 0.0 copy-start.2
  21.7 2.8 %shard_map.127.own_ref = bf16[384,384]{1,0:T(8,128)(2,1)S(1)} custom-call(f32[384,384]{1,0:T(8,128)S(1)} %bitcast.18), custom_call_target="tpu_custom_call" | custom-call | tf_op jit(solution)/shard_map/pallas_call | solution.py:268
  24.5 0.1 collective-permute-start.1
  24.5 1.3 %collective-permute-start = (bf16[384,384]{1,0:T(8,128)(2,1)S(1)}, bf16[384,384]{1,0:T(8,128)(2,1)S(1)}, u32[]{:S(2)}, u32[]{:S(2)}) collective-permute-start(bf16[384,384]{1,0:T(8,128)(2,1)S(1)} %shard_map.127.own_ref), channel_id=1, source_target_pairs={{0,1},{1,2},{2,3},{3,0},{4,5},{5,6},{6,7},{7,4},{8,9},{9,10},{10,1... | collective-permute-start | bytes 884744 | tf_op jit(solution)/shard_map/ppermute | solution.py:245
  25.9 17.5 %collective-permute-done.1.two_ref = bf16[384,384]{1,0:T(8,128)(2,1)S(1)} collective-permute-done((bf16[384,384]{1,0:T(8,128)(2,1)S(1)}, bf16[384,384]{1,0:T(8,128)(2,1)S(1)}, u32[]{:S(2)}, u32[]{:S(2)}) %collective-permute-start.1) | collective-permute-done | bytes 294944 | tf_op jit(solution)/shard_map/ppermute | solution.py:245
  43.4 3.6 %collective-permute-done.one_ref = bf16[384,384]{1,0:T(8,128)(2,1)S(1)} collective-permute-done((bf16[384,384]{1,0:T(8,128)(2,1)S(1)}, bf16[384,384]{1,0:T(8,128)(2,1)S(1)}, u32[]{:S(2)}, u32[]{:S(2)}) %collective-permute-start) | collective-permute-done | bytes 294944 | tf_op jit(solution)/shard_map/ppermute | solution.py:245
  47.0 0.0 copy-done.3
  47.0 0.0 copy-done.1
  47.0 0.0 copy-done
  47.0 0.0 copy-done.8
  47.0 0.0 copy-done.2
  47.0 0.0 copy-start.4
  47.1 1.1 %copy-done.4 = bf16[2,3,192,160]{3,2,1,0:T(8,128)(2,1)S(1)} copy-done((bf16[2,3,192,160]{3,2,1,0:T(8,128)(2,1)S(1)}, bf16[2,3,192,160]{3,2,1,0:T(8,128)(2,1)}, u32[]{:S(2)}) %copy-start.4) | copy-done | bytes 368664
  48.1 0.0 copy-start.5
  48.1 1.0 %copy-done.5 = bf16[2,288,384]{2,1,0:T(8,128)(2,1)S(1)} copy-done((bf16[2,288,384]{2,1,0:T(8,128)(2,1)S(1)}, bf16[2,288,384]{2,1,0:T(8,128)(2,1)}, u32[]{:S(2)}) %copy-start.5) | copy-done | bytes 442392
  49.1 0.0 copy-start.6
  49.1 1.0 %copy-done.6 = bf16[2,384,256]{2,1,0:T(8,128)(2,1)S(1)} copy-done((bf16[2,384,256]{2,1,0:T(8,128)(2,1)S(1)}, bf16[2,384,256]{2,1,0:T(8,128)(2,1)}, u32[]{:S(2)}) %copy-start.6) | copy-done | bytes 393240
  50.1 0.0 copy-start.7
  50.1 0.9 %copy-done.7 = bf16[2,96,192]{2,1,0:T(8,128)(2,1)S(1)} copy-done((bf16[2,96,192]{2,1,0:T(8,128)(2,1)S(1)}, bf16[2,96,192]{2,1,0:T(8,128)(2,1)}, u32[]{:S(2)}) %copy-start.7) | copy-done | bytes 73752
  51.0 10.3 %shard_map.128 = f32[2,17,17,144]{3,2,1,0:T(8,128)S(1)} custom-call(s32[2]{0:T(128)S(1)} %bitcast.19, bf16[384,384]{1,0:T(8,128)(2,1)S(1)} %shard_map.127.own_ref, bf16[384,384]{1,0:T(8,128)(2,1)S(1)} %collective-permute-done.one_ref, bf16[384,384]{1,0:T(8,128)(2,1)S(1)} %collective-permute-done.1.two_ref, bf16[2,384,768]{2,1,0:T(8,128)(2,1)S(1)} %copy-done.1, ...), custom_call_target="tpu_custom_call" | custom-call | tf_op jit(solution)/shard_map/pallas_call | solution.py:279
  61.4 1.1 %copy.14 = f32[1,1,2,17,17,144]{5,2,4,3,1,0:T(2,128)} copy(f32[1,1,2,17,17,144]{5,4,3,2,1,0:T(8,128)S(1)} %bitcast.17) | data formatting | bytes 665856 | tf_op jit(solution)/shard_map/broadcast_in_dim | solution.py:293
  (5 shorter events, 0.0 us)
Async XLA Ops:
  4.5 6.5 %copy-start.9 = (s32[1,64]{1,0:T(1,128)S(1)}, s32[1,64]{1,0:T(1,128)}, u32[]{:S(2)}) copy-start(s32[1,64]{1,0:T(1,128)} %param.15) | copy-start | bytes 772
  4.5 42.5 %copy-start.3 = (bf16[2,3,192,160]{3,2,1,0:T(8,128)(2,1)S(1)}, bf16[2,3,192,160]{3,2,1,0:T(8,128)(2,1)}, u32[]{:S(2)}) copy-start(bf16[2,3,192,160]{3,2,1,0:T(8,128)(2,1)} %constant.31.clone.frame_rows) | copy-start | bytes 1105924
  6.0 41.1 %copy-start.1 = (bf16[2,384,768]{2,1,0:T(8,128)(2,1)S(1)}, bf16[2,384,768]{2,1,0:T(8,128)(2,1)}, u32[]{:S(2)}) copy-start(bf16[2,384,768]{2,1,0:T(8,128)(2,1)} %constant.28.clone.ref_cols) | copy-start | bytes 3538948
  6.0 14.1 %all-to-all-start = ((f32[8,48,384]{2,1,0:T(8,128)}), f32[8,48,384]{2,1,0:T(8,128)}, u32[]{:S(2)}, u32[]{:S(2)}) async-start(f32[8,48,384]{2,1,0:T(8,128)} %gather_fusion), calls=%async_computation | async-start | bytes 1179648 | tf_op jit(solution)/shard_map/all_to_all | solution.py:263
  11.0 36.0 %copy-start = (bf16[2,384,768]{2,1,0:T(8,128)(2,1)S(1)}, bf16[2,384,768]{2,1,0:T(8,128)(2,1)}, u32[]{:S(2)}) copy-start(bf16[2,384,768]{2,1,0:T(8,128)(2,1)} %constant.29.clone.frame_cols) | copy-start | bytes 3538948
  11.0 36.0 %copy-start.8 = (s32[1,2]{1,0:T(1,128)S(1)}, s32[1,2]{1,0:T(1,128)}, u32[]{:S(2)}) copy-start(s32[1,2]{1,0:T(1,128)} %param.17) | copy-start | bytes 28
  21.7 25.3 %copy-start.2 = (bf16[2,3,256,256]{3,2,1,0:T(8,128)(2,1)S(1)}, bf16[2,3,256,256]{3,2,1,0:T(8,128)(2,1)}, u32[]{:S(2)}) copy-start(bf16[2,3,256,256]{3,2,1,0:T(8,128)(2,1)} %constant.33.clone.back_cols) | copy-start | bytes 2359300
  24.5 19.0 %collective-permute-start.1 = (bf16[384,384]{1,0:T(8,128)(2,1)S(1)}, bf16[384,384]{1,0:T(8,128)(2,1)S(1)}, u32[]{:S(2)}, u32[]{:S(2)}) collective-permute-start(bf16[384,384]{1,0:T(8,128)(2,1)S(1)} %shard_map.127.own_ref), channel_id=1, source_target_pairs={{0,2},{1,3},{2,0},{3,1},{4,6},{5,7},{6,4},{7,5},{8,10},{9,11},{10,... | collective-permute-start | bytes 884744 | tf_op jit(solution)/shard_map/ppermute | solution.py:245
  24.5 22.5 %collective-permute-start = (bf16[384,384]{1,0:T(8,128)(2,1)S(1)}, bf16[384,384]{1,0:T(8,128)(2,1)S(1)}, u32[]{:S(2)}, u32[]{:S(2)}) collective-permute-start(bf16[384,384]{1,0:T(8,128)(2,1)S(1)} %shard_map.127.own_ref), channel_id=1, source_target_pairs={{0,1},{1,2},{2,3},{3,0},{4,5},{5,6},{6,7},{7,4},{8,9},{9,10},{10,1... | collective-permute-start | bytes 884744 | tf_op jit(solution)/shard_map/ppermute | solution.py:245
  47.0 1.1 %copy-start.4 = (bf16[2,3,192,160]{3,2,1,0:T(8,128)(2,1)S(1)}, bf16[2,3,192,160]{3,2,1,0:T(8,128)(2,1)}, u32[]{:S(2)}) copy-start(bf16[2,3,192,160]{3,2,1,0:T(8,128)(2,1)} %constant.30.clone.ref_rows) | copy-start | bytes 1105924
  48.1 1.0 %copy-start.5 = (bf16[2,288,384]{2,1,0:T(8,128)(2,1)S(1)}, bf16[2,288,384]{2,1,0:T(8,128)(2,1)}, u32[]{:S(2)}) copy-start(bf16[2,288,384]{2,1,0:T(8,128)(2,1)} %constant.35.clone.tall) | copy-start | bytes 1327108
  49.1 1.0 %copy-start.6 = (bf16[2,384,256]{2,1,0:T(8,128)(2,1)S(1)}, bf16[2,384,256]{2,1,0:T(8,128)(2,1)}, u32[]{:S(2)}) copy-start(bf16[2,384,256]{2,1,0:T(8,128)(2,1)} %constant.34.clone.wide) | copy-start | bytes 1179652
  50.1 0.9 %copy-start.7 = (bf16[2,96,192]{2,1,0:T(8,128)(2,1)S(1)}, bf16[2,96,192]{2,1,0:T(8,128)(2,1)}, u32[]{:S(2)}) copy-start(bf16[2,96,192]{2,1,0:T(8,128)(2,1)} %constant.32.clone.back_rows) | copy-start | bytes 221188
where the time goes:
time: 63 us; the launch traced here: 62.5 us
  waiting for transfers between devices  29.1 us (46%)
  Pallas kernels  13.1 us (21%)
  local copies, waits for them, and re-layouts  8.9 us (14%)
  starting transfers between devices  6.47 us (10%)
  other arithmetic  4.76 us (8%)
    ppermute x2, waiting for transfers between devices, shifted(): lax.ppermute(x, axis, [(i, (i + by) % devices) for i in range(devices)])  21.1 us
    pallas_call x1, Pallas kernels, local(): pl.pallas_call(correlate_kernel, out_shape=jax.ShapeDtypeStruct((shifts,...  10.3 us
    all_to_all x1, waiting for transfers between devices, local(): lax.all_to_all(outgoing, 'space', split_axis=0, concat_axis=0, tiled=True)  8 us
    all_to_all x1, starting transfers between devices, local(): lax.all_to_all(outgoing, 'space', split_axis=0, concat_axis=0, tiled=True)  5.05 us
    unnamed x21, local copies, waits for them, and re-layouts  4.49 us
    unnamed x3, other arithmetic  3.13 us
    pallas_call x1, Pallas kernels, local(): pl.pallas_call(wallis_kernel, out_shape=jax.ShapeDtypeStruct((width, widt...  2.76 us
    gather x1, local copies, waits for them, and re-layouts, local(): image = incoming[order].reshape(width, width)  1.65 us
  transfers between devices with their start and end apart: 3, of which 3 were waited for; matrix products, arithmetic and copies ran while one was open for 2% of the time, Pallas kernels for 0%

commit v1 on v0

--- a/solution.py
+++ b/solution.py
@@ -27,6 +27,9 @@
 FIRST = 128 // COUNT
 F32 = jnp.float32
 BF16 = jnp.bfloat16
+MESH = pl.DeviceIdType.MESH
+TABLES = 8
+CHUNKS = 3
 
 ROW_START = (0, 112, 224)
 ROW_LEN = 160
@@ -126,30 +129,36 @@
 
 def boxed(x, box):
     a, b, c = split3(x)
-    first = dot(box, a) + dot(box, b) + dot(box, c)
-    a, b, c = split3(first)
     return dot(a, box) + dot(b, box) + dot(c, box)
 
 
-def wallis(image):
-    size = image.shape[0]
-    i = lax.broadcasted_iota(jnp.int32, (size, size), 0)
-    j = lax.broadcasted_iota(jnp.int32, (size, size), 1)
-    box = jnp.where(jnp.abs(i - j) <= WALLIS, 1.0, 0.0).astype(BF16)
-
-    def counts(k):
-        return (jnp.minimum(k, WALLIS) + jnp.minimum(size - 1 - k, WALLIS) + 1).astype(F32)
-
-    rows = counts(lax.broadcasted_iota(jnp.int32, (size, 1), 0))
-    cols = counts(lax.broadcasted_iota(jnp.int32, (1, size), 1))
-    inverse = (1.0 / rows) * (1.0 / cols)
-    center = boxed(image, box) * inverse
-    spread = boxed(image * image, box) * inverse - center * center
-    return ((image - center) * lax.rsqrt(spread + WALLIS_FLOOR)).astype(BF16)
-
-
-def wallis_kernel(image_ref, out_ref):
-    out_ref[...] = wallis(image_ref[...])
+def banded(rows, first, size):
+    i = lax.broadcasted_iota(jnp.int32, (rows, size), 0) + first
+    j = lax.broadcasted_iota(jnp.int32, (rows, size), 1)
+    return jnp.where(jnp.abs(i - j) <= WALLIS, 1.0, 0.0).astype(BF16)
+
+
+def counts(k, size):
+    return (jnp.minimum(k, WALLIS) + jnp.minimum(size - 1 - k, WALLIS) + 1).astype(F32)
+
+
+def wallis(image_ref, filtered_ref, chunk, ready):
+    size = image_ref.shape[0]
+    image = image_ref[...]
+    box = banded(size, 0, size)
+    totals = split3(boxed(image, box))
+    squares = split3(boxed(image * image, box))
+    cols = 1.0 / counts(lax.broadcasted_iota(jnp.int32, (1, size), 1), size)
+    for c in range(size // chunk):
+        first = c * chunk
+        part = banded(chunk, first, size)
+        rows = 1.0 / counts(lax.broadcasted_iota(jnp.int32, (chunk, 1), 0) + first, size)
+        inverse = rows * cols
+        center = sum(dot(part, t) for t in totals) * inverse
+        spread = sum(dot(part, t) for t in squares) * inverse - center * center
+        at = pl.ds(first, chunk)
+        filtered_ref[c] = ((image_ref[at, :] - center) * lax.rsqrt(spread + WALLIS_FLOOR)).astype(BF16)
+        ready(c)
 
 
 def spectrum(x, cols_ref, rows_ref, store):
@@ -223,73 +232,167 @@
         out_ref[k, :, v, pl.ds(128, CHIPS - 128)] = second[:LAGS, : CHIPS - 128]
 
 
-def correlate_kernel(
-    used_ref, own_ref, one_ref, two_ref,
-    ref_cols, frame_cols, ref_rows, frame_rows, back_rows, back_cols, wide, tall,
-    out_ref, ref_spec, frame_spec, ref_power, frame_power, match_ref,
+def whole_of(ref):
+    return jnp.concatenate([ref[c] for c in range(ref.shape[0])], axis=0)
+
+
+def kernel(
+    tiles, dates,
+    owner_ref, offset_ref, valid_ref, used_ref, panels_ref, *refs,
 ):
-    own = own_ref[...]
+    hbm = refs[:TABLES]
+    out_ref = refs[TABLES]
+    held = refs[TABLES + 1 : 2 * TABLES + 1]
+    (
+        stage, recv, image_ref, own_ref, one_ref, two_ref,
+        ref_spec, frame_spec, ref_power, frame_power, match_ref,
+        table_sem, panel_send, panel_recv, one_send, one_recv, two_send, two_recv,
+    ) = refs[2 * TABLES + 1 :]
+    here = lax.axis_index("space")
+    date = lax.axis_index("date")
+    right, left = lax.rem(date + 1, dates), lax.rem(date + dates - 1, dates)
+    loads = [pltpu.make_async_copy(hbm[i], held[i], table_sem.at[i]) for i in range(TABLES)]
+    for load in loads:
+        load.start()
+
+    barrier = pltpu.get_barrier_semaphore()
+    for step in range(1, tiles):
+        pl.semaphore_signal(
+            barrier, inc=1, device_id={"space": lax.rem(here + step, tiles)}, device_id_type=MESH
+        )
+    for neighbour in (left, right):
+        pl.semaphore_signal(barrier, inc=1, device_id={"date": neighbour}, device_id_type=MESH)
+
+    rows_each = panels_ref.shape[1]
+    row = lax.broadcasted_iota(jnp.int32, panels_ref.shape[1:], 0)
+
+    def masked(target):
+        pick = jnp.int32(0)
+        for i in range(tiles):
+            pick = jnp.where(owner_ref[here * tiles + i] == target, i, pick)
+        return jnp.where(row < valid_ref[here * tiles + pick], panels_ref[pick], 0.0)
+
+    recv[here] = masked(here)
+    for step in range(1, tiles):
+        stage[step - 1] = masked(lax.rem(here + step, tiles))
+    pl.semaphore_wait(barrier, tiles + 1)
+
+    def panel_copy(step, place):
+        return pltpu.make_async_remote_copy(
+            src_ref=stage.at[step - 1],
+            dst_ref=recv.at[place],
+            send_sem=panel_send.at[step - 1],
+            recv_sem=panel_recv.at[step - 1],
+            device_id={"space": lax.rem(here + step, tiles)},
+            device_id_type=MESH,
+        )
+
+    sends = [panel_copy(step, here) for step in range(1, tiles)]
+    for send in sends:
+        send.start()
+    slots = []
+    for source in range(tiles):
+        slot = jnp.int32(0)
+        for i in range(tiles):
+            at = source * tiles + i
+            slot = jnp.where(owner_ref[at] == here, offset_ref[at], slot)
+        slots.append(slot)
+    orders = []
+    for target in range(tiles):
+        order = jnp.int32(0)
+        for source in range(tiles):
+            order = jnp.where(slots[source] == target, source, order)
+        orders.append(order)
+    for step in range(1, tiles):
+        panel_copy(step, lax.rem(here + tiles - step, tiles)).wait_recv()
+    for target in range(tiles):
+        image_ref[pl.ds(target * rows_each, rows_each), :] = recv[orders[target]]
+
+    def hop(source, target, send_sem, recv_sem, c):
+        return pltpu.make_async_remote_copy(
+            src_ref=source.at[c],
+            dst_ref=target.at[c],
+            send_sem=send_sem.at[c],
+            recv_sem=recv_sem.at[c],
+            device_id={"date": right},
+            device_id_type=MESH,
+        )
+
+    chunks = own_ref.shape[0]
+    first = [hop(own_ref, one_ref, one_send, one_recv, c) for c in range(chunks)]
+    second = [hop(one_ref, two_ref, two_send, two_recv, c) for c in range(chunks)]
+    wallis(image_ref, own_ref, own_ref.shape[1], lambda c: first[c].start())
+    for send in sends:
+        send.wait_send()
+    for load in loads:
+        load.wait()
+    ref_cols, frame_cols, ref_rows, frame_rows, back_rows, back_cols, wide, tall = held
+    own = whole_of(own_ref)
     spectrum(own, ref_cols, ref_rows, ref_spec)
     ref_power[...] = powers(own, wide[1], tall[1])
-    for k, held in enumerate((one_ref, two_ref)):
-        x = held[...]
+    for c in range(chunks):
+        first[c].wait_recv()
+        second[c].start()
+
+    for k, frame_ref in enumerate((one_ref, two_ref)):
+        if k == 1:
+            for c in range(chunks):
+                second[c].wait_recv()
+        x = whole_of(frame_ref)
         spectrum(x, frame_cols, frame_rows, frame_spec)
         frame_power[...] = powers(x, wide[0], tall[0])
         used = used_ref[k].astype(F32)
         surfaces(ref_spec, frame_spec, ref_power, frame_power, used, back_rows, back_cols, match_ref)
         arrange(match_ref, out_ref, k)
-
-
-def shifted(x, axis, by):
-    devices = lax.axis_size(axis)
-    return lax.ppermute(x, axis, [(i, (i + by) % devices) for i in range(devices)])
+    for c in range(chunks):
+        first[c].wait_send()
+        second[c].wait_send()
 
 
 def local(scene_panels, panel_owner, panel_offset, panel_rows, pair_used):
     tiles = lax.axis_size("space")
-    here = lax.axis_index("space")
+    dates = lax.axis_size("date")
     panels = scene_panels[0]
     rows_each = panels.shape[1]
     width = panels.shape[2]
-    owner = panel_owner[0].reshape(tiles, tiles)
-    offset = panel_offset[0].reshape(tiles, tiles)
-    valid = panel_rows[0].reshape(tiles, tiles)
-    mine = owner[here]
-    live = (jnp.arange(rows_each)[None, :] < valid[here][:, None]).astype(jnp.float32)
-    masked = panels * live[:, :, None]
-    targets = jnp.arange(tiles, dtype=jnp.int32)
-    picks = jnp.sum(jnp.where(mine[None, :] == targets[:, None], targets[None, :], 0), axis=1)
-    outgoing = masked[picks]
-    incoming = lax.all_to_all(outgoing, "space", split_axis=0, concat_axis=0, tiled=True)
-    slot_of = jnp.sum(jnp.where(owner == here, offset, 0), axis=1)
-    order = jnp.sum(jnp.where(slot_of[None, :] == targets[:, None], targets[None, :], 0), axis=1)
-    image = incoming[order].reshape(width, width)
+    shifts = pair_used.shape[1]
+    consts = [jnp.asarray(t) for t in tables()]
     vmem = pl.BlockSpec(memory_space=pltpu.VMEM)
-    filtered = pl.pallas_call(
-        wallis_kernel,
-        out_shape=jax.ShapeDtypeStruct((width, width), BF16),
-        in_specs=[vmem],
+    smem = pl.BlockSpec(memory_space=pltpu.SMEM)
+    hbm = pl.BlockSpec(memory_space=pltpu.HBM)
+    tile = pltpu.VMEM((CHUNKS, width // CHUNKS, width), BF16)
+    spec = pltpu.VMEM((GROUPS, 2 * PER * HALF, GROUPS * 256), F32)
+    flat = pltpu.VMEM((COUNT * UPAD, 256), F32)
+    out = pl.pallas_call(
+        functools.partial(kernel, tiles, dates),
+        out_shape=jax.ShapeDtypeStruct((shifts, LAGS, LAGS, CHIPS), F32),
+        in_specs=[smem] * 4 + [vmem] + [hbm] * TABLES,
         out_specs=vmem,
-        compiler_params=pltpu.CompilerParams(vmem_limit_bytes=40 * 2**20),
-    )(image)
-    one = shifted(filtered, "date", 1)
-    two = shifted(filtered, "date", 2)
-    consts = [jnp.asarray(t) for t in tables()]
-    shifts = pair_used.shape[1]
-    out = pl.pallas_call(
-        correlate_kernel,
-        out_shape=jax.ShapeDtypeStruct((shifts, LAGS, LAGS, CHIPS), F32),
-        in_specs=[pl.BlockSpec(memory_space=pltpu.SMEM)] + [vmem] * (3 + len(consts)),
-        out_specs=vmem,
-        scratch_shapes=[
-            pltpu.VMEM((GROUPS, 2 * PER * HALF, GROUPS * 256), F32),
-            pltpu.VMEM((GROUPS, 2 * PER * HALF, GROUPS * 256), F32),
-            pltpu.VMEM((COUNT * UPAD, 256), F32),
-            pltpu.VMEM((COUNT * UPAD, 256), F32),
-            pltpu.VMEM((COUNT * UPAD, 256), F32),
+        scratch_shapes=[pltpu.VMEM(t.shape, t.dtype) for t in consts]
+        + [
+            pltpu.VMEM((tiles - 1, rows_each, width), F32),
+            pltpu.VMEM((tiles, rows_each, width), F32),
+            pltpu.VMEM((width, width), F32),
+            tile,
+            tile,
+            tile,
+            spec,
+            spec,
+            flat,
+            flat,
+            flat,
+            pltpu.SemaphoreType.DMA((TABLES,)),
+            pltpu.SemaphoreType.DMA((tiles - 1,)),
+            pltpu.SemaphoreType.DMA((tiles - 1,)),
+            pltpu.SemaphoreType.DMA((CHUNKS,)),
+            pltpu.SemaphoreType.DMA((CHUNKS,)),
+            pltpu.SemaphoreType.DMA((CHUNKS,)),
+            pltpu.SemaphoreType.DMA((CHUNKS,)),
         ],
-        compiler_params=pltpu.CompilerParams(vmem_limit_bytes=40 * 2**20),
-    )(pair_used[0], filtered, one, two, *consts)
+        compiler_params=pltpu.CompilerParams(
+            vmem_limit_bytes=40 * 2**20, collective_id=0, has_side_effects=True
+        ),
+    )(panel_owner[0], panel_offset[0], panel_rows[0], pair_used[0], panels, *consts)
     return out[None, None]
 
 

time: 63 us -> 50.6 us (0.80)
  the two profiles are of different devices: /device:TPU:19 before, /device:TPU:1 now
where the time goes in v1:
time: 50.6 us; the launch traced here: 49.8 us
  Pallas kernels  36.2 us (72%)
  local copies, waits for them, and re-layouts  13.5 us (27%)
    pallas_call x1, Pallas kernels, local(): pl.pallas_call(functools.partial(kernel, tiles, dates), out_shape=jax.Sha...  36.2 us
    unnamed x26, local copies, waits for them, and re-layouts  12.4 us
    broadcast_in_dim x1, local copies, waits for them, and re-layouts, local(): return out[None, None]  1.12 us

profile of v1, /device:TPU:1, one launch (start us, length us, event | category | flops | bytes accessed | tf_op | source)
XLA Modules:
  0.0 49.8 jit_solution(12034925045875749655)
XLA Ops:
  0.0 0.0 copy-start
  0.0 1.3 %copy-done = bf16[2,384,768]{2,1,0:T(8,128)(2,1)S(1)} copy-done((bf16[2,384,768]{2,1,0:T(8,128)(2,1)S(1)}, bf16[2,384,768]{2,1,0:T(8,128)(2,1)}, u32[]{:S(2)}) %copy-start) | copy-done | bytes 1179672
  1.3 0.0 copy-start.1
  1.3 1.3 %copy-done.1 = bf16[2,384,768]{2,1,0:T(8,128)(2,1)S(1)} copy-done((bf16[2,384,768]{2,1,0:T(8,128)(2,1)S(1)}, bf16[2,384,768]{2,1,0:T(8,128)(2,1)}, u32[]{:S(2)}) %copy-start.1) | copy-done | bytes 1179672
  2.5 0.0 copy-start.2
  2.5 1.1 %copy-done.2 = bf16[2,3,256,256]{3,2,1,0:T(8,128)(2,1)S(1)} copy-done((bf16[2,3,256,256]{3,2,1,0:T(8,128)(2,1)S(1)}, bf16[2,3,256,256]{3,2,1,0:T(8,128)(2,1)}, u32[]{:S(2)}) %copy-start.2) | copy-done | bytes 786456
  3.7 0.0 copy-start.3
  3.7 1.1 %copy-done.3 = f32[1,8,48,384]{3,2,1,0:T(8,128)S(1)} copy-done((f32[1,8,48,384]{3,2,1,0:T(8,128)S(1)}, f32[1,8,48,384]{3,2,1,0:T(8,128)}, u32[]{:S(2)}) %copy-start.3) | copy-done | bytes 589848
  4.7 0.0 copy-start.4
  4.7 1.1 %copy-done.4 = bf16[2,3,192,160]{3,2,1,0:T(8,128)(2,1)S(1)} copy-done((bf16[2,3,192,160]{3,2,1,0:T(8,128)(2,1)S(1)}, bf16[2,3,192,160]{3,2,1,0:T(8,128)(2,1)}, u32[]{:S(2)}) %copy-start.4) | copy-done | bytes 368664
  5.8 0.0 copy-start.5
  5.8 1.1 %copy-done.5 = bf16[2,3,192,160]{3,2,1,0:T(8,128)(2,1)S(1)} copy-done((bf16[2,3,192,160]{3,2,1,0:T(8,128)(2,1)S(1)}, bf16[2,3,192,160]{3,2,1,0:T(8,128)(2,1)}, u32[]{:S(2)}) %copy-start.5) | copy-done | bytes 368664
  6.9 0.0 copy-start.6
  6.9 1.0 %copy-done.6 = bf16[2,288,384]{2,1,0:T(8,128)(2,1)S(1)} copy-done((bf16[2,288,384]{2,1,0:T(8,128)(2,1)S(1)}, bf16[2,288,384]{2,1,0:T(8,128)(2,1)}, u32[]{:S(2)}) %copy-start.6) | copy-done | bytes 442392
  7.9 0.0 copy-start.7
  7.9 1.0 %copy-done.7 = bf16[2,384,256]{2,1,0:T(8,128)(2,1)S(1)} copy-done((bf16[2,384,256]{2,1,0:T(8,128)(2,1)S(1)}, bf16[2,384,256]{2,1,0:T(8,128)(2,1)}, u32[]{:S(2)}) %copy-start.7) | copy-done | bytes 393240
  8.9 0.0 copy-start.8
  8.9 0.9 %copy-done.8 = bf16[2,96,192]{2,1,0:T(8,128)(2,1)S(1)} copy-done((bf16[2,96,192]{2,1,0:T(8,128)(2,1)S(1)}, bf16[2,96,192]{2,1,0:T(8,128)(2,1)}, u32[]{:S(2)}) %copy-start.8) | copy-done | bytes 73752
  9.8 0.0 copy-start.9
  9.8 0.7 %copy-done.9 = s32[1,64]{1,0:T(1,128)S(1)} copy-done((s32[1,64]{1,0:T(1,128)S(1)}, s32[1,64]{1,0:T(1,128)}, u32[]{:S(2)}) %copy-start.9) | copy-done | bytes 280
  10.4 0.0 copy-start.10
  10.4 0.7 %copy-done.10 = s32[1,64]{1,0:T(1,128)S(1)} copy-done((s32[1,64]{1,0:T(1,128)S(1)}, s32[1,64]{1,0:T(1,128)}, u32[]{:S(2)}) %copy-start.10) | copy-done | bytes 280
  11.1 0.0 copy-start.11
  11.1 0.7 %copy-done.11 = s32[1,64]{1,0:T(1,128)S(1)} copy-done((s32[1,64]{1,0:T(1,128)S(1)}, s32[1,64]{1,0:T(1,128)}, u32[]{:S(2)}) %copy-start.11) | copy-done | bytes 280
  11.7 0.0 copy-start.12
  11.7 0.7 %copy-done.12 = s32[1,2]{1,0:T(1,128)S(1)} copy-done((s32[1,2]{1,0:T(1,128)S(1)}, s32[1,2]{1,0:T(1,128)}, u32[]{:S(2)}) %copy-start.12) | copy-done | bytes 32
  12.4 36.2 %shard_map.127 = f32[2,17,17,144]{3,2,1,0:T(8,128)S(1)} custom-call(s32[64]{0:T(128)S(1)} %bitcast.8, s32[64]{0:T(128)S(1)} %bitcast.9, s32[64]{0:T(128)S(1)} %bitcast.10, s32[2]{0:T(128)S(1)} %bitcast.11, f32[8,48,384]{2,1,0:T(8,128)S(1)} %bitcast.7, bf16[2,384,768]{2,1,0:T(8,128)(2,1)S(1)} %copy-done.1, bf16[2,384,768]{2,1,0:T(8,128)(2,1)S(1)} %copy-done, ...), custom_call_target="tpu_custom_call" | custom-call | tf_op jit(solution)/shard_map/pallas_call | solution.py:366
  48.6 1.1 %copy.14 = f32[1,1,2,17,17,144]{5,2,4,3,1,0:T(2,128)} copy(f32[1,1,2,17,17,144]{5,4,3,2,1,0:T(8,128)S(1)} %bitcast.6) | data formatting | bytes 665856 | tf_op jit(solution)/shard_map/broadcast_in_dim | solution.py:396
Async XLA Ops:
  0.0 1.3 %copy-start = (bf16[2,384,768]{2,1,0:T(8,128)(2,1)S(1)}, bf16[2,384,768]{2,1,0:T(8,128)(2,1)}, u32[]{:S(2)}) copy-start(bf16[2,384,768]{2,1,0:T(8,128)(2,1)} %constant.17.clone.refs_1_) | copy-start | bytes 3538948
  1.3 1.3 %copy-start.1 = (bf16[2,384,768]{2,1,0:T(8,128)(2,1)S(1)}, bf16[2,384,768]{2,1,0:T(8,128)(2,1)}, u32[]{:S(2)}) copy-start(bf16[2,384,768]{2,1,0:T(8,128)(2,1)} %constant.16.clone.refs_0_) | copy-start | bytes 3538948
  2.5 1.1 %copy-start.2 = (bf16[2,3,256,256]{3,2,1,0:T(8,128)(2,1)S(1)}, bf16[2,3,256,256]{3,2,1,0:T(8,128)(2,1)}, u32[]{:S(2)}) copy-start(bf16[2,3,256,256]{3,2,1,0:T(8,128)(2,1)} %constant.21.clone.refs_5_) | copy-start | bytes 2359300
  3.7 1.1 %copy-start.3 = (f32[1,8,48,384]{3,2,1,0:T(8,128)S(1)}, f32[1,8,48,384]{3,2,1,0:T(8,128)}, u32[]{:S(2)}) copy-start(f32[1,8,48,384]{3,2,1,0:T(8,128)} %param.13) | copy-start | bytes 1769476
  4.7 1.1 %copy-start.4 = (bf16[2,3,192,160]{3,2,1,0:T(8,128)(2,1)S(1)}, bf16[2,3,192,160]{3,2,1,0:T(8,128)(2,1)}, u32[]{:S(2)}) copy-start(bf16[2,3,192,160]{3,2,1,0:T(8,128)(2,1)} %constant.19.clone.refs_3_) | copy-start | bytes 1105924
  5.8 1.1 %copy-start.5 = (bf16[2,3,192,160]{3,2,1,0:T(8,128)(2,1)S(1)}, bf16[2,3,192,160]{3,2,1,0:T(8,128)(2,1)}, u32[]{:S(2)}) copy-start(bf16[2,3,192,160]{3,2,1,0:T(8,128)(2,1)} %constant.18.clone.refs_2_) | copy-start | bytes 1105924
  6.9 1.0 %copy-start.6 = (bf16[2,288,384]{2,1,0:T(8,128)(2,1)S(1)}, bf16[2,288,384]{2,1,0:T(8,128)(2,1)}, u32[]{:S(2)}) copy-start(bf16[2,288,384]{2,1,0:T(8,128)(2,1)} %constant.23.clone.refs_7_) | copy-start | bytes 1327108
  7.9 1.0 %copy-start.7 = (bf16[2,384,256]{2,1,0:T(8,128)(2,1)S(1)}, bf16[2,384,256]{2,1,0:T(8,128)(2,1)}, u32[]{:S(2)}) copy-start(bf16[2,384,256]{2,1,0:T(8,128)(2,1)} %constant.22.clone.refs_6_) | copy-start | bytes 1179652
  8.9 0.9 %copy-start.8 = (bf16[2,96,192]{2,1,0:T(8,128)(2,1)S(1)}, bf16[2,96,192]{2,1,0:T(8,128)(2,1)}, u32[]{:S(2)}) copy-start(bf16[2,96,192]{2,1,0:T(8,128)(2,1)} %constant.20.clone.refs_4_) | copy-start | bytes 221188
  9.8 0.7 %copy-start.9 = (s32[1,64]{1,0:T(1,128)S(1)}, s32[1,64]{1,0:T(1,128)}, u32[]{:S(2)}) copy-start(s32[1,64]{1,0:T(1,128)} %param.14) | copy-start | bytes 772
  10.4 0.7 %copy-start.10 = (s32[1,64]{1,0:T(1,128)S(1)}, s32[1,64]{1,0:T(1,128)}, u32[]{:S(2)}) copy-start(s32[1,64]{1,0:T(1,128)} %param.15) | copy-start | bytes 772
  11.1 0.7 %copy-start.11 = (s32[1,64]{1,0:T(1,128)S(1)}, s32[1,64]{1,0:T(1,128)}, u32[]{:S(2)}) copy-start(s32[1,64]{1,0:T(1,128)} %param.16) | copy-start | bytes 772
  11.7 0.7 %copy-start.12 = (s32[1,2]{1,0:T(1,128)S(1)}, s32[1,2]{1,0:T(1,128)}, u32[]{:S(2)}) copy-start(s32[1,2]{1,0:T(1,128)} %param.17) | copy-start | bytes 28

commit v2 on v1

--- a/solution.py
+++ b/solution.py
@@ -29,7 +29,7 @@
 BF16 = jnp.bfloat16
 MESH = pl.DeviceIdType.MESH
 TABLES = 8
-CHUNKS = 3
+CHUNKS = 6
 
 ROW_START = (0, 112, 224)
 ROW_LEN = 160
@@ -91,14 +91,17 @@
             back_cols[g, base : base + HALF, lane_of(v, cj)] = np.sin(omega * v)
 
     wide = np.zeros((2, TILE, 256))
-    tall = np.zeros((2, COUNT * UPAD, TILE))
+    tall = np.zeros((2, GROUPS, PER * UPAD, ROW_LEN))
     for c in range(COUNT):
         for v in range(LAGS):
             start = CHIP * c + v - SEARCH
             wide[0, max(start, 0) : max(start + CHIP, 0), lane_of(v, c)] = 1
-            tall[0, c * UPAD + v, max(start, 0) : max(start + CHIP, 0)] = 1
+            h, q = divmod(c, PER)
+            low, high = max(start, 0) - ROW_START[h], min(start + CHIP, TILE) - ROW_START[h]
+            tall[0, h, q * UPAD + v, low:high] = 1
             wide[1, CHIP * c : CHIP * c + CHIP, lane_of(v, c)] = 1
-            tall[1, c * UPAD + v, CHIP * c : CHIP * c + CHIP] = 1
+            low = CHIP * c - ROW_START[h]
+            tall[1, h, q * UPAD + v, low : low + CHIP] = 1
     return (
         split_host(columns(SEARCH, SEARCH + CHIP)),
         split_host(columns(0, FRAME)),
@@ -161,31 +164,33 @@
         ready(c)
 
 
-def spectrum(x, cols_ref, rows_ref, store):
-    parts = []
+def across(x, cols_ref, wide, z_ref, e_ref, at):
     for g in range(GROUPS):
-        at = pl.ds(COL_START[g], COL_LEN[g])
+        cols = pl.ds(COL_START[g], COL_LEN[g])
         piece = x[:, COL_START[g] : COL_START[g] + COL_LEN[g]]
         lanes = pl.ds(g * 256, 256)
-        z = dot(piece, cols_ref[0, at, lanes]) + dot(piece, cols_ref[1, at, lanes])
-        hi, lo = split(z)
-        for h in range(GROUPS):
-            s = ROW_START[h]
-            zh, zl = hi[s : s + ROW_LEN], lo[s : s + ROW_LEN]
-            store[h, :, lanes] = dot(rows_ref[0, h], zh) + dot(rows_ref[0, h], zl) + dot(rows_ref[1, h], zh)
-
-
-def powers(x, wide, tall):
+        hi, lo = split(dot(piece, cols_ref[0, cols, lanes]) + dot(piece, cols_ref[1, cols, lanes]))
+        z_ref[0, at, lanes], z_ref[1, at, lanes] = hi, lo
     wide_f = x.astype(F32)
     hi, lo = split(wide_f * wide_f)
     hi, lo = split(dot(hi, wide) + dot(lo, wide))
-    return dot(tall, hi) + dot(tall, lo)
-
-
-def surfaces(ref_spec, frame_spec, ref_power, frame_power, used, back_rows, back_cols, match_ref):
+    e_ref[0, at, :], e_ref[1, at, :] = hi, lo
+
+
+def down(h, rows_ref, tall, z_ref, e_ref, spec, power):
+    at = pl.ds(ROW_START[h], ROW_LEN)
+    for g in range(GROUPS):
+        lanes = pl.ds(g * 256, 256)
+        zh, zl = z_ref[0, at, lanes], z_ref[1, at, lanes]
+        spec[h, :, lanes] = dot(rows_ref[0, h], zh) + dot(rows_ref[0, h], zl) + dot(rows_ref[1, h], zh)
+    out = pl.ds(h * PER * UPAD, PER * UPAD)
+    power[out, :] = dot(tall[h], e_ref[0, at, :]) + dot(tall[h], e_ref[1, at, :])
+
+
+def surfaces(group, ref_spec, frame_spec, ref_power, frame_power, used, back_rows, back_cols, match_ref):
     mid = PER * HALF
     area = float(CHIP * CHIP)
-    for h in range(GROUPS):
+    for h in (group,):
         total = None
         for g in range(GROUPS):
             even, odd = pl.ds(g * 256, 128), pl.ds(g * 256 + 128, 128)
@@ -232,10 +237,6 @@
         out_ref[k, :, v, pl.ds(128, CHIPS - 128)] = second[:LAGS, : CHIPS - 128]
 
 
-def whole_of(ref):
-    return jnp.concatenate([ref[c] for c in range(ref.shape[0])], axis=0)
-
-
 def kernel(
     tiles, dates,
     owner_ref, offset_ref, valid_ref, used_ref, panels_ref, *refs,
@@ -245,7 +246,7 @@
     held = refs[TABLES + 1 : 2 * TABLES + 1]
     (
         stage, recv, image_ref, own_ref, one_ref, two_ref,
-        ref_spec, frame_spec, ref_power, frame_power, match_ref,
+        ref_spec, frame_spec, ref_power, frame_power, match_ref, z_ref, e_ref,
         table_sem, panel_send, panel_recv, one_send, one_recv, two_send, two_recv,
     ) = refs[2 * TABLES + 1 :]
     here = lax.axis_index("space")
@@ -327,22 +328,28 @@
     for load in loads:
         load.wait()
     ref_cols, frame_cols, ref_rows, frame_rows, back_rows, back_cols, wide, tall = held
-    own = whole_of(own_ref)
-    spectrum(own, ref_cols, ref_rows, ref_spec)
-    ref_power[...] = powers(own, wide[1], tall[1])
+    chunk = own_ref.shape[1]
+    for c in range(chunks):
+        across(own_ref[c], ref_cols, wide[1], z_ref, e_ref, pl.ds(c * chunk, chunk))
+    for h in range(GROUPS):
+        down(h, ref_rows, tall.at[1], z_ref, e_ref, ref_spec, ref_power)
     for c in range(chunks):
         first[c].wait_recv()
         second[c].start()
 
     for k, frame_ref in enumerate((one_ref, two_ref)):
-        if k == 1:
-            for c in range(chunks):
+        used = used_ref[k].astype(F32)
+        done = 0
+        for c in range(chunks):
+            if k == 1:
                 second[c].wait_recv()
-        x = whole_of(frame_ref)
-        spectrum(x, frame_cols, frame_rows, frame_spec)
-        frame_power[...] = powers(x, wide[0], tall[0])
-        used = used_ref[k].astype(F32)
-        surfaces(ref_spec, frame_spec, ref_power, frame_power, used, back_rows, back_cols, match_ref)
+            across(frame_ref[c], frame_cols, wide[0], z_ref, e_ref, pl.ds(c * chunk, chunk))
+            while done < GROUPS and ROW_START[done] + ROW_LEN <= (c + 1) * chunk:
+                down(done, frame_rows, tall.at[0], z_ref, e_ref, frame_spec, frame_power)
+                surfaces(
+                    done, ref_spec, frame_spec, ref_power, frame_power, used, back_rows, back_cols, match_ref
+                )
+                done += 1
         arrange(match_ref, out_ref, k)
     for c in range(chunks):
         first[c].wait_send()
@@ -381,6 +388,8 @@
             flat,
             flat,
             flat,
+            pltpu.VMEM((2, width, GROUPS * 256), BF16),
+            pltpu.VMEM((2, width, 256), BF16),
             pltpu.SemaphoreType.DMA((TABLES,)),
             pltpu.SemaphoreType.DMA((tiles - 1,)),
             pltpu.SemaphoreType.DMA((tiles - 1,)),
@@ -390,7 +399,7 @@
             pltpu.SemaphoreType.DMA((CHUNKS,)),
         ],
         compiler_params=pltpu.CompilerParams(
-            vmem_limit_bytes=40 * 2**20, collective_id=0, has_side_effects=True
+            vmem_limit_bytes=64 * 2**20 - 2**16, collective_id=0, has_side_effects=True
         ),
     )(panel_owner[0], panel_offset[0], panel_rows[0], pair_used[0], panels, *consts)
     return out[None, None]

time: 50.6 us -> 37.6 us (0.74); the launches traced: 49.8 us -> 37.4 us
  local copies, waits for them, and re-layouts: 13.5 us -> 2.27 us
  Pallas kernels: 36.2 us -> 35.1 us
    unnamed x26 -> x0, local copies, waits for them, and re-layouts: 12.4 us -> none
    broadcast_in_dim x1, local copies, waits for them, and re-layouts: 1.12 us -> 2.27 us  [local(): return out[None, None]]
    pallas_call x1, Pallas kernels: 36.2 us -> 35.1 us  [local(): pl.pallas_call(functools.partial(kernel, tiles, dates), out_shape=jax.Sha...]
where the time goes in v2:
time: 37.6 us; the launch traced here: 37.4 us
  Pallas kernels  35.1 us (93%)
  local copies, waits for them, and re-layouts  2.27 us (6%)
    pallas_call x1, Pallas kernels, local(): pl.pallas_call(functools.partial(kernel, tiles, dates), out_shape=jax.Sha...  35.1 us
    broadcast_in_dim x1, local copies, waits for them, and re-layouts, local(): return out[None, None]  2.27 us

profile of v2, /device:TPU:1, one launch (start us, length us, event | category | flops | bytes accessed | tf_op | source)
XLA Modules:
  0.0 37.4 jit_solution(9135770963936656685)
XLA Ops:
  0.0 35.1 %shard_map.127 = f32[2,17,17,144]{3,2,1,0:T(8,128)} custom-call(s32[64]{0:T(128)} %bitcast.8, s32[64]{0:T(128)} %bitcast.9, s32[64]{0:T(128)} %bitcast.10, s32[2]{0:T(128)} %bitcast.11, f32[8,48,384]{2,1,0:T(8,128)} %bitcast.7, bf16[2,384,768]{2,1,0:T(8,128)(2,1)} %constant.16.clone.refs_0_, bf16[2,384,768]{2,1,0:T(8,128)(2,1)} %constant.17.clone.refs_1_, ...), custom_call_target="tpu_custom_call" | custom-call | tf_op jit(solution)/shard_map/pallas_call | solution.py:373
  35.1 2.3 %copy.14 = f32[1,1,2,17,17,144]{5,2,4,3,1,0:T(2,128)} copy(f32[1,1,2,17,17,144]{5,4,3,2,1,0:T(8,128)} %bitcast.6) | data formatting | bytes 665856 | tf_op jit(solution)/shard_map/broadcast_in_dim | solution.py:405

commit v3 on v2

--- a/solution.py
+++ b/solution.py
@@ -154,11 +154,12 @@
     cols = 1.0 / counts(lax.broadcasted_iota(jnp.int32, (1, size), 1), size)
     for c in range(size // chunk):
         first = c * chunk
-        part = banded(chunk, first, size)
+        low, high = max(0, first - 16), min(size, first + chunk + 16)
+        part = banded(chunk, first - low, high - low)
         rows = 1.0 / counts(lax.broadcasted_iota(jnp.int32, (chunk, 1), 0) + first, size)
         inverse = rows * cols
-        center = sum(dot(part, t) for t in totals) * inverse
-        spread = sum(dot(part, t) for t in squares) * inverse - center * center
+        center = sum(dot(part, t[low:high]) for t in totals) * inverse
+        spread = sum(dot(part, t[low:high]) for t in squares) * inverse - center * center
         at = pl.ds(first, chunk)
         filtered_ref[c] = ((image_ref[at, :] - center) * lax.rsqrt(spread + WALLIS_FLOOR)).astype(BF16)
         ready(c)

time: 37.6 us -> 37.4 us (level)
  no operation moved by 1% of the time
where the time goes in v3:
time: 37.4 us; the launch traced here: 37.2 us
  Pallas kernels  34.9 us (93%)
  local copies, waits for them, and re-layouts  2.27 us (6%)
    pallas_call x1, Pallas kernels, local(): pl.pallas_call(functools.partial(kernel, tiles, dates), out_shape=jax.Sha...  34.9 us
    broadcast_in_dim x1, local copies, waits for them, and re-layouts, local(): return out[None, None]  2.27 us

profile of v3, /device:TPU:1, one launch (start us, length us, event | category | flops | bytes accessed | tf_op | source)
XLA Modules:
  0.0 37.2 jit_solution(3772282633315849453)
XLA Ops:
  0.0 34.9 %shard_map.127 = f32[2,17,17,144]{3,2,1,0:T(8,128)} custom-call(s32[64]{0:T(128)} %bitcast.8, s32[64]{0:T(128)} %bitcast.9, s32[64]{0:T(128)} %bitcast.10, s32[2]{0:T(128)} %bitcast.11, f32[8,48,384]{2,1,0:T(8,128)} %bitcast.7, bf16[2,384,768]{2,1,0:T(8,128)(2,1)} %constant.16.clone.refs_0_, bf16[2,384,768]{2,1,0:T(8,128)(2,1)} %constant.17.clone.refs_1_, ...), custom_call_target="tpu_custom_call" | custom-call | tf_op jit(solution)/shard_map/pallas_call | solution.py:374
  34.9 2.3 %copy.14 = f32[1,1,2,17,17,144]{5,2,4,3,1,0:T(2,128)} copy(f32[1,1,2,17,17,144]{5,4,3,2,1,0:T(8,128)} %bitcast.6) | data formatting | bytes 665856 | tf_op jit(solution)/shard_map/broadcast_in_dim | solution.py:406
